TPU v7x, 32 devices: a whole 2x2x4 slice. The times are simulated.
32 devices in a mesh: row: 8 (over y, x, core), col: 4 (over z).
Axes of the slice: x: 2, y: 2, z: 4, core: 2. Of those that a mesh axis runs over, the one named last changes fastest.
Arguments:
- hidden_in: bfloat16 [2048, 7168], P('row'), may hold values from -6 to 6
- norm_gain: float32 [7168], replicated, may hold values from 0.5 to 1.5
- norm_bias: float32 [7168], replicated, may hold values from -3 to 3
- w_query: bfloat16 [7168, 6144], P('row', 'col'), may hold values from -0.0625 to 0.0625
- w_keyval: bfloat16 [7168, 2, 6144], P('row', None, 'col'), may hold values from -0.125 to 0.125
- bias_query: float32 [6144], P('col'), may hold values from -3 to 3
- bias_keyval: float32 [2, 6144], P(None, 'col'), may hold values from -3 to 3
- cache_keys: bfloat16 [8, 4096, 6144], P('row', None, 'col'), may hold values from -60 to 60
- cache_values: bfloat16 [8, 4096, 6144], P('row', None, 'col'), may hold values from -12 to 12
- cache_lengths: int32 [8], replicated, may hold values from 2 to 4096
- owner_slot: int32 [8], replicated, may hold values from 0 to 7, each once
- w_out: bfloat16 [6144, 7168], P('col', 'row'), may hold values from -0.3125 to 0.3125
- bias_out: float32 [7168], P('col'), may hold values from -3 to 3
Outputs:
- hidden_out: bfloat16 [2048, 7168], P('row', 'col')
- new_keys: bfloat16 [8, 256, 6144], P('row', None, 'col')
- new_values: bfloat16 [8, 256, 6144], P('row', None, 'col')
Inputs may be any that keep to these rules, and one draw needn't show every extreme that they name: `owner_slot`: each slot is the owner of exactly one request.
All inputs are finite; a program needn't handle non-finite values.
Results may differ from a plain program's by a relative error of at most 0.01375.
Values may be sent and summed in bfloat16 or wider, within the bound.
No kernel may reach another device: no remote copies, remote signals or barrier semaphores. Data moves between devices by JAX's collectives and lax.ppermute only.
A program may use at most 192 MiB of HBM per device.

v0:
```python
import functools

import jax
import jax.numpy as jnp
from jax import lax
from jax.experimental import pallas as pl
from jax.experimental.pallas import tpu as pltpu
from jax.sharding import PartitionSpec as P

HEAD = 128
F32 = jnp.float32
MIB = 1024 * 1024
SMALL = pl.CostEstimate(flops=1, bytes_accessed=1, transcendentals=0)
BF16 = jnp.bfloat16


def normalize_kernel(meta_ref, hidden_ref, gain_ref, bias_ref, *out_refs):
    piece_refs = out_refs
    width = hidden_ref.shape[1]
    length = piece_refs[0].shape[1]
    rows = hidden_ref[...].astype(F32)
    mean = jnp.sum(rows, axis=1, keepdims=True) / width
    centered = rows - mean
    var = jnp.sum(centered * centered, axis=1, keepdims=True) / width
    factor = lax.rsqrt(var + 1e-05)
    for d, ref in enumerate(piece_refs):
        part = pl.ds(pl.multiple_of((meta_ref[0] ^ d) * length, HEAD), length)
        ref[...] = ((hidden_ref[:, part].astype(F32) - mean) * factor * gain_ref[:, part] + bias_ref[:, part]).astype(BF16)


def normalize(meta, hidden, gain, bias, pairs):
    rows, width = hidden.shape
    step = 32
    whole = pl.BlockSpec((1, width), lambda i, meta: (0, 0))
    return pl.pallas_call(
        normalize_kernel,
        out_shape=[jax.ShapeDtypeStruct((rows, width // pairs), BF16)] * pairs,
        grid_spec=pltpu.PrefetchScalarGridSpec(
            num_scalar_prefetch=1,
            grid=(rows // step,),
            in_specs=[pl.BlockSpec((step, width), lambda i, meta: (i, 0)), whole, whole],
            out_specs=[pl.BlockSpec((step, width // pairs), lambda i, meta: (i, 0))] * pairs,
        ),
        compiler_params=pltpu.CompilerParams(vmem_limit_bytes=60 * MIB),
        cost_estimate=SMALL,
    )(meta, hidden, gain[None], bias[None])


def weave_kernel(meta_ref, q_ref, kv_ref, taken_q_ref, taken_kv_ref, *refs, cuts, behind):
    (out_ref,) = refs[behind:]

    def weave(queries_ref, keyval_ref):
        at = 0
        for first, last in cuts:
            for kind in range(3):
                cols = pl.ds(first * HEAD, (last - first) * HEAD)
                part = queries_ref[:, cols] if kind == 0 else keyval_ref[:, kind - 1, cols]
                out_ref[:, pl.ds(at, (last - first) * HEAD)] = part
                at += (last - first) * HEAD

    @pl.when(pl.program_id(0) == 0)
    def _():
        weave(q_ref, kv_ref)

    @pl.when(pl.program_id(0) != 0)
    def _():
        weave(taken_q_ref, taken_kv_ref)


def weave(core, w_query, w_keyval, taken_query, taken_keyval, cuts, behind):
    rows, cols = w_query.shape
    half = cols // 2
    step = 128 if rows % 128 == 0 else 64
    steps = rows // step
    own = lambda side, i, meta: jnp.where(side == 0, i, steps - 1)
    other = lambda side, i, meta: jnp.where(side == 0, 0, i)
    specs = []
    for place in (own, other):
        specs.append(pl.BlockSpec((step, half), lambda side, i, meta, place=place: (place(side, i, meta), meta[0])))
        specs.append(pl.BlockSpec((step, 2, half), lambda side, i, meta, place=place: (place(side, i, meta), 0, meta[0])))
    return pl.pallas_call(
        functools.partial(weave_kernel, cuts=cuts, behind=len(behind)),
        out_shape=jax.ShapeDtypeStruct((2 * rows, 3 * half), BF16),
        grid_spec=pltpu.PrefetchScalarGridSpec(
            num_scalar_prefetch=1,
            grid=(2, steps),
            in_specs=specs + [pl.BlockSpec(memory_space=pl.ANY)] * len(behind),
            out_specs=pl.BlockSpec((step, 3 * half), lambda side, i, meta: ((meta[0] ^ side) * steps + i, 0)),
        ),
        compiler_params=pltpu.CompilerParams(vmem_limit_bytes=40 * MIB),
        cost_estimate=SMALL,
    )(core.reshape(1).astype(jnp.int32), w_query, w_keyval, taken_query, taken_keyval, *behind)


def fetch_kernel(*refs, count, behind):
    out_refs, sem = refs[count + behind : -1], refs[-1]
    copies = [pltpu.make_async_copy(refs[at], out_refs[at], sem.at[at]) for at in range(count)]
    for copy in copies:
        copy.start()
    for copy in copies:
        copy.wait()


def fetch(sources, behind):
    space = pl.BlockSpec(memory_space=pl.ANY)
    return pl.pallas_call(
        functools.partial(fetch_kernel, count=len(sources), behind=len(behind)),
        out_shape=[jax.ShapeDtypeStruct(source.shape, source.dtype) for source in sources],
        in_specs=[space] * (len(sources) + len(behind)),
        out_specs=[pl.BlockSpec(memory_space=pltpu.VMEM)] * len(sources),
        scratch_shapes=[pltpu.SemaphoreType.DMA((len(sources),))],
        cost_estimate=SMALL,
    )(*sources, *behind)


def swap(value, axis, mask, size):
    return lax.ppermute(value, axis, [(i, i ^ mask) for i in range(size)])


def gather_block(table, places, dst, sem):
    for at, place in enumerate(places):

        @pl.when(table == at)
        def _(place=place):
            pltpu.make_async_copy(place, dst, sem).start()


def project_kernel(meta_ref, *refs, blocks, group, orders, behind):
    x_refs, w_ref = refs[:blocks], refs[blocks]
    out_refs, (x_buf, w_buf, x_sem, w_sem) = refs[blocks + 1 + behind : -4], refs[-4:]
    cols = w_buf.shape[1] // 3
    load = pltpu.make_async_copy(w_ref.at[:, pl.ds(group * 3 * cols, 3 * cols)], w_buf, w_sem)
    load.start()
    sequence = sorted(range(blocks), key=lambda e: -sum(bool(e >> order[0] & 1) for order in orders))
    for at, e in enumerate(sequence):
        gather_block(meta_ref[e], x_refs, x_buf.at[at], x_sem.at[at])
    load.wait()
    group_len = x_buf.shape[1]
    batch = 2
    for start in range(0, blocks, batch):
        for at in range(start, start + batch):
            pltpu.make_async_copy(x_refs[0], x_buf.at[at], x_sem.at[at]).wait()
        tokens = x_buf[start : start + batch].reshape(batch * group_len, x_buf.shape[2])
        product = jnp.dot(tokens, w_buf[...], preferred_element_type=F32).astype(BF16)
        first = 0
        for p, order in enumerate(orders):
            keep_ref, send_ref = out_refs[2 * p], out_refs[2 * p + 1]
            count = keep_ref.shape[2] // (3 * HEAD)
            ranked = slots_in(blocks, order)
            for c in range(batch):
                place = ranked.index(sequence[start + c])
                ref = keep_ref if place < blocks // 2 else send_ref
                for h in range(count):
                    for kind in range(3):
                        at = kind * cols + (first + h) * HEAD
                        ref[place % (blocks // 2), :, pl.ds((3 * h + kind) * HEAD, HEAD)] = product[
                            c * group_len : (c + 1) * group_len, at : at + HEAD
                        ]
            first += count


def slots_in(blocks, order):
    return sorted(range(blocks), key=lambda e: [e >> bit & 1 for bit in order] + [e & 1])


def project(meta, x_blocks, weights, group, per_group, orders, counts, behind):
    blocks = len(x_blocks)
    group_len, depth = x_blocks[0].shape
    any_space = pl.BlockSpec(memory_space=pl.ANY)
    out_shape = []
    for count in counts:
        out_shape += [jax.ShapeDtypeStruct((blocks // 2, group_len, count * 3 * HEAD), BF16)] * 2
    cols = per_group * 3 * HEAD
    return pl.pallas_call(
        functools.partial(project_kernel, blocks=blocks, group=group, orders=orders, behind=len(behind)),
        out_shape=out_shape,
        in_specs=[pl.BlockSpec(memory_space=pltpu.SMEM)] + [any_space] * (blocks + 1 + len(behind)),
        out_specs=[pl.BlockSpec(memory_space=pltpu.VMEM)] * len(out_shape),
        scratch_shapes=[
            pltpu.VMEM((blocks, group_len, depth), BF16),
            pltpu.VMEM((depth, cols), BF16),
            pltpu.SemaphoreType.DMA((blocks,)),
            pltpu.SemaphoreType.DMA(()),
        ],
        compiler_params=pltpu.CompilerParams(vmem_limit_bytes=60 * MIB),
        cost_estimate=SMALL,
    )(meta, *x_blocks, weights, *behind)


def forward_kernel(*refs, parts, terms, behind):
    out_refs = refs[parts * terms + behind :]
    for p in range(parts):
        mine = refs[p * terms : (p + 1) * terms]
        out_refs[p][...] = sum(ref[...].astype(F32) for ref in mine).astype(BF16)


def forward(terms, behind):
    left = min(t.shape[0] for t in terms[0]) // 2
    shapes = [(left, *ts[0].shape[1:]) for ts in terms]
    specs = [pl.BlockSpec(shape, lambda i: (1, 0, 0)) for shape, ts in zip(shapes, terms) for _ in ts]
    return pl.pallas_call(
        functools.partial(forward_kernel, parts=len(terms), terms=len(terms[0]), behind=len(behind)),
        grid=(1,),
        out_shape=[jax.ShapeDtypeStruct(shape, BF16) for shape in shapes],
        in_specs=specs + [pl.BlockSpec(memory_space=pl.ANY)] * len(behind),
        out_specs=[pl.BlockSpec(shape, lambda i: (0, 0, 0)) for shape in shapes],
        compiler_params=pltpu.CompilerParams(vmem_limit_bytes=24 * MIB),
        cost_estimate=SMALL,
    )(*[t for ts in terms for t in ts], *behind)


def settle_kernel(bias_ref, scale_ref, *refs, parts, terms, behind):
    mine_ref, theirs_ref = refs[parts * terms + behind :]
    width = mine_ref.shape[2]
    head = 0
    for p in range(parts):
        for h in range(refs[p * terms].shape[2] // width):
            cols = pl.ds(h * width, width)
            for e, ref in enumerate((mine_ref, theirs_ref)):
                total = sum(t[e, :, cols].astype(F32) for t in refs[p * terms : (p + 1) * terms])
                ref[head] = ((total + bias_ref[head : head + 1, :]) * scale_ref[...]).astype(BF16)
            head += 1


def settle(terms, bias, scale, behind):
    heads, width = bias.shape
    rows = terms[0][0].shape[1]
    specs = [pl.BlockSpec((2, *t.shape[1:]), lambda i: (0, 0, 0)) for ts in terms for t in ts]
    whole = pl.BlockSpec((heads, rows, width), lambda i: (0, 0, 0))
    return pl.pallas_call(
        functools.partial(settle_kernel, parts=len(terms), terms=len(terms[0]), behind=len(behind)),
        grid=(1,),
        out_shape=[jax.ShapeDtypeStruct((heads, rows, width), BF16)] * 2,
        in_specs=[pl.BlockSpec((heads, width), lambda i: (0, 0)), pl.BlockSpec((1, width), lambda i: (0, 0))]
        + specs
        + [pl.BlockSpec(memory_space=pl.ANY)] * len(behind),
        out_specs=[whole, whole],
        compiler_params=pltpu.CompilerParams(vmem_limit_bytes=24 * MIB),
        cost_estimate=SMALL,
    )(bias, scale, *[t for ts in terms for t in ts], *behind)


def attend_kernel(meta_ref, own_ref, other_ref, k_ref, v_ref, *refs, key_len, behind):
    o_ref, nk_ref, nv_ref = refs[behind:]
    length = meta_ref[0]
    qkv = jnp.where(pl.program_id(0) < pl.num_programs(0) // 2, own_ref[0], other_ref[0])
    q, new_k, new_v = qkv[:, :HEAD], qkv[:, HEAD : 2 * HEAD], qkv[:, 2 * HEAD :]
    nk_ref[...] = new_k
    nv_ref[...] = new_v
    group = q.shape[0]
    cache_len = k_ref.shape[1]

    def scores_of(at):
        keys = k_ref[0, at : at + key_len, :]
        scores = lax.dot_general(q, keys, (((1,), (1,)), ((), ())), preferred_element_type=F32)
        positions = at + lax.broadcasted_iota(jnp.int32, (1, key_len), 1)
        return jnp.where(positions < length, scores, -1e30)

    def lane_sum(probs):
        total = probs[:, :HEAD]
        for at in range(HEAD, probs.shape[1], HEAD):
            total = total + probs[:, at : at + HEAD]
        return total

    rows = lax.broadcasted_iota(jnp.int32, (group, group), 0)
    cols = lax.broadcasted_iota(jnp.int32, (group, group), 1)
    scores = lax.dot_general(q, new_k, (((1,), (1,)), ((), ())), preferred_element_type=F32)
    scores = jnp.where(cols <= rows, scores, -1e30)
    following = scores_of(0)
    row_max = jnp.max(scores, axis=1, keepdims=True)
    probs = jnp.exp(scores - row_max)
    row_sum = lane_sum(probs)
    weighted = jnp.dot(probs.astype(BF16), new_v, preferred_element_type=F32)
    for at in range(0, cache_len, key_len):
        scores = following
        if at + key_len < cache_len:
            following = scores_of(at + key_len)
        new_max = jnp.maximum(row_max, jnp.max(scores, axis=1, keepdims=True))
        factor = jnp.exp(row_max - new_max)
        probs = jnp.exp(scores - new_max)
        row_max = new_max
        row_sum = row_sum * factor + lane_sum(probs)
        values = v_ref[0, at : at + key_len, :]
        weighted = weighted * factor + jnp.dot(probs.astype(BF16), values, preferred_element_type=F32)
    total = jnp.sum(row_sum, axis=1, keepdims=True)
    o_ref[...] = (weighted / total).astype(BF16)


def attend(meta, own, other, cache_k, cache_v, base, half, behind):
    count, group, width = own.shape
    heads = 2 * count
    cache_len = cache_k.shape[1]
    key_len = min(512, cache_len)

    def side(i, meta):
        return (i // count) ^ meta[1]

    cached = pl.BlockSpec((1, cache_len, HEAD), lambda i, meta: (0, 0, side(i, meta) * half + base + i % count))
    placed = pl.BlockSpec((group, HEAD), lambda i, meta: (0, side(i, meta) * count + i % count))
    return pl.pallas_call(
        functools.partial(attend_kernel, key_len=key_len, behind=len(behind)),
        out_shape=[jax.ShapeDtypeStruct((group, heads * HEAD), BF16)] * 3,
        grid_spec=pltpu.PrefetchScalarGridSpec(
            num_scalar_prefetch=1,
            grid=(heads,),
            in_specs=[
                pl.BlockSpec((1, group, width), lambda i, meta: (jnp.minimum(i, count - 1), 0, 0)),
                pl.BlockSpec((1, group, width), lambda i, meta: (jnp.maximum(i - count, 0), 0, 0)),
                cached,
                cached,
            ]
            + [pl.BlockSpec(memory_space=pl.ANY)] * len(behind),
            out_specs=[placed] * 3,
        ),
        compiler_params=pltpu.CompilerParams(vmem_limit_bytes=60 * MIB),
        cost_estimate=SMALL,
    )(meta, own, other, cache_k, cache_v, *behind)


def output_kernel(*refs, pairs, groups):
    a_refs = [refs[g * pairs : (g + 1) * pairs] for g in range(groups)]
    w_refs = refs[groups * pairs : groups * pairs + 2]
    out_refs, (buf, sem) = refs[groups * pairs + 2 : -2], refs[-2:]
    _, rows, head_cols = buf.shape
    half = head_cols // 2
    cols = half // groups
    chunk = rows // len(out_refs)
    for d in range(pairs):
        for g in range(groups):
            for side in range(2):
                pltpu.make_async_copy(
                    a_refs[g][d].at[:, pl.ds(side * cols, cols)],
                    buf.at[d, :, pl.ds(side * half + g * cols, cols)],
                    sem.at[d],
                ).start()
    for d in range(pairs):
        pltpu.make_async_copy(buf.at[d], buf.at[d], sem.at[d]).wait()
    for d in range(0, pairs, 2):
        tokens = buf[d : d + 2].reshape(2 * rows, head_cols)
        for j in range(2):
            product = jnp.dot(tokens, w_refs[j][...], preferred_element_type=F32).astype(BF16)
            for c, out_ref in enumerate(out_refs):
                for at in range(2):
                    first = at * rows + c * chunk
                    out_ref[j, d + at] = product[first : first + chunk]


def output(gathered, w_pair, chunks):
    groups, pairs = len(gathered), len(gathered[0])
    rows = gathered[0][0].shape[0]
    head_cols, out_cols = w_pair[0].shape
    space = pl.BlockSpec(memory_space=pl.ANY)
    vmem = pl.BlockSpec(memory_space=pltpu.VMEM)
    return pl.pallas_call(
        functools.partial(output_kernel, pairs=pairs, groups=groups),
        out_shape=[jax.ShapeDtypeStruct((2, pairs, rows // chunks, out_cols), BF16)] * chunks,
        in_specs=[space] * (groups * pairs) + [vmem] * 2,
        out_specs=[vmem] * chunks,
        scratch_shapes=[pltpu.VMEM((pairs, rows, head_cols), BF16), pltpu.SemaphoreType.DMA((pairs,))],
        compiler_params=pltpu.CompilerParams(vmem_limit_bytes=40 * MIB),
        cost_estimate=SMALL,
    )(*[a for part in gathered for a in part], *w_pair)


def block_call(kernel, out_shapes, scalars, arrays, shapes, indices, behind):
    return pl.pallas_call(
        functools.partial(kernel, behind=len(behind)),
        out_shape=[jax.ShapeDtypeStruct(shape, BF16) for shape in out_shapes],
        grid_spec=pltpu.PrefetchScalarGridSpec(
            num_scalar_prefetch=1,
            grid=(1,),
            in_specs=[pl.BlockSpec(shape, index) for shape, index in zip(shapes, indices)]
            + [pl.BlockSpec(memory_space=pl.ANY)] * len(behind),
            out_specs=[
                pl.BlockSpec(shape, lambda i, meta, rank=len(shape): (0,) * rank) for shape in out_shapes
            ],
        ),
        compiler_params=pltpu.CompilerParams(vmem_limit_bytes=16 * MIB),
        cost_estimate=SMALL,
    )(scalars, *arrays, *behind)


def split_pair_kernel(meta_ref, own_ref, came_ref, *refs, behind):
    mine_ref, sent_ref = refs[behind:]
    count = mine_ref.shape[1]
    pairs = 2 * count
    offsets = slots_in(2 * pairs, range(1, pairs.bit_length()))[::2]
    for at, e in enumerate(offsets):
        place = meta_ref[e]
        for j in range(2):
            block = jnp.where(place % 2 == 0, own_ref[j, place // 2], came_ref[1 - j, place // 2])
            if at < count:
                mine_ref[j, at] = block
            else:
                sent_ref[j, at - count] = block


def split_pair(places, own, came, behind):
    _, pairs, chunk, cols = own.shape
    first = lambda i, meta: (0, 0, 0, 0)
    shapes = [(2, pairs // 2, chunk, cols)] * 2
    return block_call(split_pair_kernel, shapes, places, [own, came], [own.shape] * 2, [first] * 2, behind)


def choose_kernel(meta_ref, keep_ref, came_ref, *refs, behind):
    mine_ref, sent_ref = refs[behind:]

    @pl.when(meta_ref[0] == 0)
    def _():
        mine_ref[...] = keep_ref[...]
        sent_ref[...] = came_ref[...]

    @pl.when(meta_ref[0] != 0)
    def _():
        mine_ref[...] = came_ref[...]
        sent_ref[...] = keep_ref[...]


def choose(flip, keep, came, behind):
    first = lambda i, meta: (0,) * keep.ndim
    return block_call(choose_kernel, [keep.shape] * 2, flip, [keep, came], [keep.shape] * 2, [first] * 2, behind)


def add_split_kernel(meta_ref, keep_ref, came_ref, *refs, behind):
    mine_ref, sent_ref = refs[behind:]
    count = mine_ref.shape[1]
    total = (keep_ref[...].astype(F32) + came_ref[...].astype(F32)).astype(BF16)
    mine_ref[...] = total[:, :count]
    sent_ref[...] = total[:, count:]


def add_split(keep, came, behind):
    slices, count, chunk, cols = keep.shape
    first = lambda i, meta: (0, 0, 0, 0)
    shapes = [(slices, count // 2, chunk, cols)] * 2
    scalars = jnp.zeros((1,), jnp.int32)
    return block_call(add_split_kernel, shapes, scalars, [keep, came], [keep.shape] * 2, [first] * 2, behind)


def finish_rows_kernel(meta_ref, keep_ref, came_ref, hidden_ref, bias_ref, *refs, behind):
    (out_ref,) = refs[behind:]
    cols = keep_ref.shape[3]
    total = [keep_ref[j, 0].astype(F32) + came_ref[j, 0].astype(F32) for j in range(2)]
    for side in range(2):
        at = pl.ds(side * cols, cols)
        part = jnp.where(meta_ref[0] == side, total[0], total[1])
        out_ref[:, at] = (part + bias_ref[:, at] + hidden_ref[:, at].astype(F32)).astype(BF16)


def finish_rows(meta, keep, came, hidden, bias, at, behind):
    chunk, cols = keep.shape[2:]
    width = 2 * cols
    shapes = [keep.shape, keep.shape, (chunk, width), (1, width)]
    first = lambda i, meta: (0, 0, 0, 0)
    indices = [first, first, lambda i, meta: (at, meta[1]), lambda i, meta: (0, 0)]
    arrays = [keep, came, hidden, bias[None]]
    return block_call(finish_rows_kernel, [(chunk, width)], meta, arrays, shapes, indices, behind)[0]


def local(
    rows_n,
    cols_n,
    hidden_in,
    norm_gain,
    norm_bias,
    w_query,
    w_keyval,
    bias_query,
    bias_keyval,
    cache_keys,
    cache_values,
    cache_lengths,
    owner_slot,
    w_out,
    bias_out,
):
    row = lax.axis_index("row")
    col = lax.axis_index("col")
    core = row & 1
    group_len, width = hidden_in.shape
    slice_len, head_cols = w_query.shape
    half = head_cols // HEAD // 2
    half_cols = head_cols // 2
    pairs = rows_n // 2
    row_bits = rows_n.bit_length() - 1
    col_bits = cols_n.bit_length() - 1
    q_scale = HEAD ** (-0.5)
    slot_ids = jnp.arange(rows_n, dtype=jnp.int32)
    is_owner = owner_slot[:, None] == slot_ids[None, :]
    inverse = jnp.sum(jnp.where(is_owner, slot_ids[:, None], 0), axis=0).astype(jnp.int32)

    pair = row // 2
    pieces = normalize(pair.reshape(1).astype(jnp.int32), hidden_in, norm_gain, norm_bias, pairs)
    x_blocks = [None] * rows_n
    for offset in reversed(range(pairs)):
        piece = swap(pieces[offset], "row", 2 * offset, rows_n) if offset else pieces[0]
        x_blocks[2 * offset] = piece

    groups = 3 if half % 3 == 0 else 1
    per_group = half // groups
    parts = [(g * per_group, (g + 1) * per_group) for g in range(groups)]
    taken = swap(w_query, "row", 1, rows_n), swap(w_keyval, "row", 1, rows_n)
    weights = weave(core, w_query, w_keyval, *taken, parts, [pieces[0]])
    w_pair = w_out, swap(w_out, "row", 1, rows_n)
    arrived = fetch(x_blocks[2::2], [weights, w_pair[1]])
    for offset in range(pairs):
        x_blocks[2 * offset + 1] = swap(arrived[offset - 1] if offset else x_blocks[0], "row", 1, rows_n)

    bias = jnp.concatenate([bias_query[None], bias_keyval], axis=0).reshape(3, 2, half, HEAD).transpose(1, 2, 0, 3)
    bias = lax.dynamic_index_in_dim(bias, core, 0, keepdims=False).reshape(half, 3 * HEAD)
    scale = jnp.concatenate([jnp.full((HEAD,), q_scale, F32), jnp.ones((2 * HEAD,), F32)])

    counts = [per_group // 2, per_group - per_group // 2] if per_group > 1 else [1]
    pair_bits = list(range(1, row_bits))
    orders = [pair_bits[at % len(pair_bits) :] + pair_bits[: at % len(pair_bits)] for at in range(len(counts))]
    project_meta = (inverse[row ^ slot_ids] ^ row).astype(jnp.int32)
    attend_meta = jnp.stack([cache_lengths[inverse[row]], core]).astype(jnp.int32)

    def project_group(g, behind):
        return project(project_meta, x_blocks, weights, g, per_group, orders, counts, behind)

    projected = [project_group(0, [])]
    key_parts, value_parts, gathered, finished, waiting = [], [], [], [], []

    def finish(g):
        base = g * per_group
        mine, theirs = settle(
            waiting[g],
            bias[base : base + per_group],
            scale[None],
            finished[-1:] + ([projected[g + 2][0]] if g + 2 < groups else []),
        )
        came = swap(theirs, "row", 1, rows_n)
        attended, new_k, new_v = attend(
            attend_meta, mine, came, cache_keys, cache_values, base, half, gathered[0][1:] if g == 1 else []
        )
        finished.append(attended)
        key_parts.append(new_k)
        value_parts.append(new_v)
        gathered.append([swap(attended, "row", 2 * d, rows_n) if d else attended for d in range(pairs)])

    for g in range(groups):
        terms = [[projected[g][2 * p]] for p in range(len(orders))]
        sends = [projected[g][2 * p + 1] for p in range(len(orders))]
        if g + 1 < groups:
            projected.append(project_group(g + 1, [sent] if g else [projected[0][0]]))
        for at in range(len(pair_bits)):
            for p, order in enumerate(orders):
                terms[p].append(swap(sends[p], "row", 1 << order[at], rows_n))
            if at + 1 < len(pair_bits):
                sends = forward(terms, finished[-1:] + ([projected[g + 1][0]] if g + 1 < groups else []))
                sent = sends[0]
        waiting.append(terms)
        if g:
            finish(g - 1)
    finish(groups - 1)

    cols = per_group * HEAD
    new_k, new_v = (
        jnp.concatenate([p[:, side * cols : (side + 1) * cols] for side in range(2) for p in parts], axis=1)[None]
        for parts in (key_parts, value_parts)
    )

    places = (owner_slot[row ^ slot_ids] ^ row).astype(jnp.int32)
    shift = row_bits - col_bits
    if shift != 1:
        raise ValueError("unexpected mesh")
    chunks = 4
    chunk = group_len // chunks
    last = row_bits - 1
    flips = [((row >> bit) ^ (col >> (bit - 1))) & 1 for bit in range(1, row_bits)]
    flips = [flip.reshape(1).astype(jnp.int32) for flip in flips]
    final_meta = jnp.stack([core, col]).astype(jnp.int32)
    late = [0, 0] + [at for bit in range(1, last) for at in (4.5 * bit + 1.5, 4.5 * bit + 4.5)]
    late += [4.5 * last + 1.5, 4.5 * last + 4.6]
    order = sorted((c * (2 if step > 1 else 0.5) + late[step], step, c) for c in range(chunks) for step in range(1, 2 * last + 2))
    products = output(gathered, w_pair, chunks)
    state = {c: (product, swap(product, "row", 1, rows_n)) for c, product in enumerate(products)}
    done, order_behind = {}, []
    for _, step, c in order:
        if step == 2 * last + 1:
            done[c] = finish_rows(final_meta, *state[c], hidden_in, bias_out, c, order_behind)
            order_behind = [done[c]]
        else:
            bit = (step + 1) // 2
            if step == 1:
                keep, sent = split_pair(places, *state[c], order_behind)
            elif step % 2:
                keep, sent = add_split(*state[c], order_behind)
            else:
                keep, sent = choose(flips[bit - 1], *state[c], order_behind)
            axis, mask, size = ("row", 1 << bit, rows_n) if step % 2 else ("col", 1 << (bit - 1), cols_n)
            state[c] = (keep, swap(sent, axis, mask, size))
            order_behind = [sent]
    hidden_out = jnp.concatenate([done[c] for c in range(chunks)], axis=0)
    return hidden_out, new_k, new_v


def solution(mesh):
    placed = (
        P("row", None),
        P(),
        P(),
        P("row", "col"),
        P("row", None, "col"),
        P("col"),
        P(None, "col"),
        P("row", None, "col"),
        P("row", None, "col"),
        P(),
        P(),
        P("col", "row"),
        P("col"),
    )
    return jax.shard_map(
        functools.partial(local, mesh.shape["row"], mesh.shape["col"]),
        mesh=mesh,
        in_specs=placed,
        out_specs=(P("row", "col"), P("row", None, "col"), P("row", None, "col")),
        check_vma=False,
    )
```

profile of v0, /device:TPU:0, one launch (start us, length us, event | category | flops | bytes accessed | tf_op | source)
XLA Modules:
  0.0 343.6 jit_solution(9575022227204873632)
XLA Ops:
  1.7 7.8 %shard_map.148 = (bf16[256,1792]{1,0:T(8,128)(2,1)}, bf16[256,1792]{1,0:T(8,128)(2,1)}, bf16[256,1792]{1,0:T(8,128)(2,1)}, bf16[256,1792]{1,0:T(8,128)(2,1)}) custom-call(s32[1]{0:T(128)} %bitcast.8.meta_ref, bf16[256,7168]{1,0:T(8,128)(2,1)} %hidden_ref.9, f32[1,7168]{1,0:T(1,128)} %bitcast.20, f32[1,7168]{1,0:T(1,128)} %bitcast.21), custom_call_target="tpu_custom_call" | custom-call | flops 1 | bytes 1 | tf_op jit(solution)/shard_map/pallas_call | solution.py:35
  13.6 4.5 %collective-permute-done.4.taken_q_ref = bf16[896,1536]{1,0:T(8,128)(2,1)} collective-permute-done((bf16[896,1536]{1,0:T(8,128)(2,1)}, bf16[896,1536]{1,0:T(8,128)(2,1)}, u32[]{:S(2)}, u32[]{:S(2)}) %collective-permute-start.4) | collective-permute-done | bytes 2752544 | tf_op jit(solution)/shard_map/ppermute | solution.py:117
  18.0 3.8 %collective-permute-start.3 = (bf16[256,1792]{1,0:T(8,128)(2,1)}, bf16[256,1792]{1,0:T(8,128)(2,1)}, u32[]{:S(2)}, u32[]{:S(2)}) collective-permute-start(bf16[256,1792]{1,0:T(8,128)(2,1)} %get-tuple-element.82), channel_id=1, source_target_pairs={{0,24},{4,28},{8,16},{12,20},{16,8},{20,12},{24,0},{28,4},{1,25},{... | collective-permute-start | bytes 2752520 | tf_op jit(solution)/shard_map/ppermute | solution.py:117
  27.4 16.1 %shard_map.149.refs_3_.refs_8_ = bf16[1792,2304]{1,0:T(8,128)(2,1)} custom-call(s32[1]{0:T(128)} %bitcast.meta_ref, bf16[896,1536]{1,0:T(8,128)(2,1)S(1)} %copy-done.20, bf16[896,2,1536]{2,1,0:T(2,128)(2,1)S(1)} %copy-done.9, bf16[896,1536]{1,0:T(8,128)(2,1)} %collective-permute-done.4.taken_q_ref, ...), custom_call_target="tpu_custom_call" | custom-call | flops 1 | bytes 1 | tf_op jit(solution)/shard_map/pallas_call | solution.py:81
  43.5 10.9 %collective-permute-done.2.refs_1_.refs_4_ = bf16[256,1792]{1,0:T(8,128)(2,1)} collective-permute-done((bf16[256,1792]{1,0:T(8,128)(2,1)}, bf16[256,1792]{1,0:T(8,128)(2,1)}, u32[]{:S(2)}, u32[]{:S(2)}) %collective-permute-start.2) | collective-permute-done | bytes 917536 | tf_op jit(solution)/shard_map/ppermute | solution.py:117
  65.7 14.1 %shard_map.151 = (bf16[4,256,384]{2,1,0:T(8,128)(2,1)}, bf16[4,256,384]{2,1,0:T(8,128)(2,1)}, bf16[4,256,384]{2,1,0:T(8,128)(2,1)}, bf16[4,256,384]{2,1,0:T(8,128)(2,1)}) custom-call(s32[8]{0:T(128)} %broadcast_xor_fusion.meta_ref, bf16[256,1792]{1,0:T(8,128)(2,1)} %get-tuple-element.79.refs_0_, bf16[256,1792]{1,0:T(8,128)(2,1)} %collective-permute-done.refs_1_, ...), custom_call_target="tpu_custom_call" | custom-call | flops 1 | bytes 1 | tf_op jit(solution)/shard_map/pallas_call | solution.py:174
  81.9 14.2 %shard_map.152 = (bf16[4,256,384]{2,1,0:T(8,128)(2,1)}, bf16[4,256,384]{2,1,0:T(8,128)(2,1)}, bf16[4,256,384]{2,1,0:T(8,128)(2,1)}, bf16[4,256,384]{2,1,0:T(8,128)(2,1)}) custom-call(s32[8]{0:T(128)} %broadcast_xor_fusion.meta_ref, bf16[256,1792]{1,0:T(8,128)(2,1)} %get-tuple-element.79.refs_0_, bf16[256,1792]{1,0:T(8,128)(2,1)} %collective-permute-done.refs_1_, ...), custom_call_target="tpu_custom_call" | custom-call | flops 1 | bytes 1 | tf_op jit(solution)/shard_map/pallas_call | solution.py:174
  96.2 3.5 %collective-permute-done.10.refs_1_ = bf16[4,256,384]{2,1,0:T(8,128)(2,1)S(1)} collective-permute-done((bf16[4,256,384]{2,1,0:T(8,128)(2,1)}, bf16[4,256,384]{2,1,0:T(8,128)(2,1)S(1)}, u32[]{:S(2)}, u32[]{:S(2)}) %collective-permute-start.10) | collective-permute-done | bytes 786464 | tf_op jit(solution)/shard_map/ppermute | solution.py:117
  108.3 14.4 %shard_map.154 = (bf16[4,256,384]{2,1,0:T(8,128)(2,1)}, bf16[4,256,384]{2,1,0:T(8,128)(2,1)}, bf16[4,256,384]{2,1,0:T(8,128)(2,1)}, bf16[4,256,384]{2,1,0:T(8,128)(2,1)}) custom-call(s32[8]{0:T(128)} %broadcast_xor_fusion.meta_ref, bf16[256,1792]{1,0:T(8,128)(2,1)} %get-tuple-element.79.refs_0_, bf16[256,1792]{1,0:T(8,128)(2,1)} %collective-permute-done.refs_1_, ...), custom_call_target="tpu_custom_call" | custom-call | flops 1 | bytes 1 | tf_op jit(solution)/shard_map/pallas_call | solution.py:174
  125.1 7.7 %collective-permute-done.13.refs_5_ = bf16[2,256,384]{2,1,0:T(8,128)(2,1)S(1)} collective-permute-done((bf16[2,256,384]{2,1,0:T(8,128)(2,1)}, bf16[2,256,384]{2,1,0:T(8,128)(2,1)S(1)}, u32[]{:S(2)}, u32[]{:S(2)}) %collective-permute-start.13) | collective-permute-done | bytes 393248 | tf_op jit(solution)/shard_map/ppermute | solution.py:117
  150.7 10.5 %shard_map.156 = (bf16[256,512]{1,0:T(8,128)(2,1)}, bf16[256,512]{1,0:T(8,128)(2,1)}, bf16[256,512]{1,0:T(8,128)(2,1)}) custom-call(s32[2]{0:T(128)} %pad_add_fusion.1.meta_ref, bf16[2,256,384]{2,1,0:T(8,128)(2,1)} %copy-done.37, bf16[2,256,384]{2,1,0:T(8,128)(2,1)} %collective-permute-done.14.other_ref, bf16[1,4096,1536]{2,1,0:T(8,128)(2,1)} %k_ref.5, ...), custom_call_target="tpu_custom_call" | custom-call | flops 1 | bytes 1 | tf_op jit(solution)/shard_map/pallas_call | solution.py:300
  172.8 18.6 %collective-permute-done.16.refs_1_.refs_2_ = bf16[256,512]{1,0:T(8,128)(2,1)S(1)} collective-permute-done((bf16[256,512]{1,0:T(8,128)(2,1)S(1)}, bf16[256,512]{1,0:T(8,128)(2,1)S(1)}, u32[]{:S(2)}, u32[]{:S(2)}) %collective-permute-start.16) | collective-permute-done | bytes 262176 | tf_op jit(solution)/shard_map/ppermute | solution.py:117
  192.3 10.6 %shard_map.159 = (bf16[256,512]{1,0:T(8,128)(2,1)}, bf16[256,512]{1,0:T(8,128)(2,1)}, bf16[256,512]{1,0:T(8,128)(2,1)}) custom-call(s32[2]{0:T(128)} %pad_add_fusion.1.meta_ref, bf16[2,256,384]{2,1,0:T(8,128)(2,1)} %copy-done.38, bf16[2,256,384]{2,1,0:T(8,128)(2,1)} %copy-done.49, bf16[1,4096,1536]{2,1,0:T(8,128)(2,1)} %k_ref.5, ...), custom_call_target="tpu_custom_call" | custom-call | flops 1 | bytes 1 | tf_op jit(solution)/shard_map/pallas_call | solution.py:300
  209.3 11.0 %shard_map.162 = (bf16[256,512]{1,0:T(8,128)(2,1)}, bf16[256,512]{1,0:T(8,128)(2,1)}, bf16[256,512]{1,0:T(8,128)(2,1)}) custom-call(s32[2]{0:T(128)} %pad_add_fusion.1.meta_ref, bf16[2,256,384]{2,1,0:T(8,128)(2,1)} %copy-done.40, bf16[2,256,384]{2,1,0:T(8,128)(2,1)} %copy-done.50, bf16[1,4096,1536]{2,1,0:T(8,128)(2,1)} %k_ref.5, bf16[1,4096,1536]{2,1,0:T(8,128)(2,1)} %v_ref.5), custom_call_target="tpu_custom_call" | custom-call | flops 1 | bytes 1 | tf_op jit(solution)/shard_map/pallas_call | solution.py:300
  223.8 5.9 %collective-permute-done.31.refs_9_ = bf16[256,512]{1,0:T(8,128)(2,1)S(1)} collective-permute-done((bf16[256,512]{1,0:T(8,128)(2,1)}, bf16[256,512]{1,0:T(8,128)(2,1)S(1)}, u32[]{:S(2)}, u32[]{:S(2)}) %collective-permute-start.31) | collective-permute-done | bytes 262176 | tf_op jit(solution)/shard_map/ppermute | solution.py:117
  229.7 4.8 %collective-permute-done.32.refs_10_ = bf16[256,512]{1,0:T(8,128)(2,1)S(1)} collective-permute-done((bf16[256,512]{1,0:T(8,128)(2,1)}, bf16[256,512]{1,0:T(8,128)(2,1)S(1)}, u32[]{:S(2)}, u32[]{:S(2)}) %collective-permute-start.32) | collective-permute-done | bytes 262176 | tf_op jit(solution)/shard_map/ppermute | solution.py:117
  237.3 8.8 %shard_map.163 = (bf16[2,4,64,896]{3,2,1,0:T(8,128)(2,1)}, bf16[2,4,64,896]{3,2,1,0:T(8,128)(2,1)S(1)}, bf16[2,4,64,896]{3,2,1,0:T(8,128)(2,1)S(1)}, bf16[2,4,64,896]{3,2,1,0:T(8,128)(2,1)S(1)}) custom-call(bf16[256,512]{1,0:T(8,128)(2,1)S(1)} %copy-done.22, bf16[256,512]{1,0:T(8,128)(2,1)S(1)} %copy-done.24, bf16[256,512]{1,0:T(8,128)(2,1)S(1)} %copy-done.26, ...), custom_call_target="tpu_custom_call" | custom-call | flops 1 | bytes 1 | tf_op jit(solution)/shard_map/pallas_call | solution.py:354
  260.6 7.9 %collective-permute-done.35.came_ref = bf16[2,2,64,896]{3,2,1,0:T(8,128)(2,1)S(1)} collective-permute-done((bf16[2,2,64,896]{3,2,1,0:T(8,128)(2,1)S(1)}, bf16[2,2,64,896]{3,2,1,0:T(8,128)(2,1)S(1)}, u32[]{:S(2)}, u32[]{:S(2)}) %collective-permute-start.35) | collective-permute-done | bytes 458784 | tf_op jit(solution)/shard_map/ppermute | solution.py:117
  271.5 6.8 %collective-permute-done.40.came_ref = bf16[2,2,64,896]{3,2,1,0:T(8,128)(2,1)S(1)} collective-permute-done((bf16[2,2,64,896]{3,2,1,0:T(8,128)(2,1)S(1)}, bf16[2,2,64,896]{3,2,1,0:T(8,128)(2,1)S(1)}, u32[]{:S(2)}, u32[]{:S(2)}) %collective-permute-start.40) | collective-permute-done | bytes 458784 | tf_op jit(solution)/shard_map/ppermute | solution.py:117
  281.7 6.4 %collective-permute-done.42.came_ref = bf16[2,2,64,896]{3,2,1,0:T(8,128)(2,1)S(1)} collective-permute-done((bf16[2,2,64,896]{3,2,1,0:T(8,128)(2,1)S(1)}, bf16[2,2,64,896]{3,2,1,0:T(8,128)(2,1)S(1)}, u32[]{:S(2)}, u32[]{:S(2)}) %collective-permute-start.42) | collective-permute-done | bytes 458784 | tf_op jit(solution)/shard_map/ppermute | solution.py:117
  291.6 5.4 %collective-permute-done.47.came_ref = bf16[2,2,64,896]{3,2,1,0:T(8,128)(2,1)S(1)} collective-permute-done((bf16[2,2,64,896]{3,2,1,0:T(8,128)(2,1)S(1)}, bf16[2,2,64,896]{3,2,1,0:T(8,128)(2,1)S(1)}, u32[]{:S(2)}, u32[]{:S(2)}) %collective-permute-start.47) | collective-permute-done | bytes 458784 | tf_op jit(solution)/shard_map/ppermute | solution.py:117
  303.6 11.1 %collective-permute-done.43.came_ref = bf16[2,1,64,896]{3,2,1,0:T(8,128)(2,1)S(1)} collective-permute-done((bf16[2,1,64,896]{3,2,1,0:T(8,128)(2,1)S(1)}, bf16[2,1,64,896]{3,2,1,0:T(8,128)(2,1)S(1)}, u32[]{:S(2)}, u32[]{:S(2)}) %collective-permute-start.43) | collective-permute-done | bytes 229408 | tf_op jit(solution)/shard_map/ppermute | solution.py:117
  325.6 11.5 %collective-permute-done.51.came_ref = bf16[2,1,64,896]{3,2,1,0:T(8,128)(2,1)S(1)} collective-permute-done((bf16[2,1,64,896]{3,2,1,0:T(8,128)(2,1)S(1)}, bf16[2,1,64,896]{3,2,1,0:T(8,128)(2,1)S(1)}, u32[]{:S(2)}, u32[]{:S(2)}) %collective-permute-start.51) | collective-permute-done | bytes 229408 | tf_op jit(solution)/shard_map/ppermute | solution.py:117
  337.8 3.6 %collective-permute-done.53.came_ref = bf16[2,1,64,896]{3,2,1,0:T(8,128)(2,1)S(1)} collective-permute-done((bf16[2,1,64,896]{3,2,1,0:T(8,128)(2,1)S(1)}, bf16[2,1,64,896]{3,2,1,0:T(8,128)(2,1)S(1)}, u32[]{:S(2)}, u32[]{:S(2)}) %collective-permute-start.53) | collective-permute-done | bytes 229408 | tf_op jit(solution)/shard_map/ppermute | solution.py:117
  (276 shorter events, 120.0 us)
Async XLA Ops:
  0.6 21.2 %collective-permute-start.5 = (bf16[896,2,1536]{2,1,0:T(2,128)(2,1)}, bf16[896,2,1536]{2,1,0:T(2,128)(2,1)}, u32[]{:S(2)}, u32[]{:S(2)}) collective-permute-start(bf16[896,2,1536]{2,1,0:T(2,128)(2,1)} %kv_ref.1), channel_id=1, source_target_pairs={{0,4},{4,0},{8,12},{12,8},{16,20},{20,16},{24,28},{28,24},{1,5},{5... | collective-permute-start | bytes 16515080 | tf_op jit(solution)/shard_map/ppermute | solution.py:117
  1.2 53.2 %collective-permute-start.6 = (bf16[1536,896]{1,0:T(8,128)(2,1)}, bf16[1536,896]{1,0:T(8,128)(2,1)S(1)}, u32[]{:S(2)}, u32[]{:S(2)}) collective-permute-start(bf16[1536,896]{1,0:T(8,128)(2,1)} %refs_12_.1), channel_id=1, source_target_pairs={{0,4},{4,0},{8,12},{12,8},{16,20},{20,16},{24,28},{28,24},{1,5},{5... | collective-permute-start | bytes 8257544 | tf_op jit(solution)/shard_map/ppermute | solution.py:117
  9.5 34.1 %collective-permute-start.1 = (bf16[256,1792]{1,0:T(8,128)(2,1)}, bf16[256,1792]{1,0:T(8,128)(2,1)}, u32[]{:S(2)}, u32[]{:S(2)}) collective-permute-start(bf16[256,1792]{1,0:T(8,128)(2,1)} %get-tuple-element.80), channel_id=1, source_target_pairs={{0,8},{4,12},{8,0},{12,4},{16,24},{20,28},{24,16},{28,20},{1,9},{5... | collective-permute-start | bytes 2752520 | tf_op jit(solution)/shard_map/ppermute | solution.py:117
  12.0 42.4 %collective-permute-start.2 = (bf16[256,1792]{1,0:T(8,128)(2,1)}, bf16[256,1792]{1,0:T(8,128)(2,1)}, u32[]{:S(2)}, u32[]{:S(2)}) collective-permute-start(bf16[256,1792]{1,0:T(8,128)(2,1)} %get-tuple-element.81), channel_id=1, source_target_pairs={{0,16},{4,20},{8,24},{12,28},{16,0},{20,4},{24,8},{28,12},{1,17},{... | collective-permute-start | bytes 2752520 | tf_op jit(solution)/shard_map/ppermute | solution.py:117
  18.0 36.4 %collective-permute-start.3 = (bf16[256,1792]{1,0:T(8,128)(2,1)}, bf16[256,1792]{1,0:T(8,128)(2,1)}, u32[]{:S(2)}, u32[]{:S(2)}) collective-permute-start(bf16[256,1792]{1,0:T(8,128)(2,1)} %get-tuple-element.82), channel_id=1, source_target_pairs={{0,24},{4,28},{8,16},{12,20},{16,8},{20,12},{24,0},{28,4},{1,25},{... | collective-permute-start | bytes 2752520 | tf_op jit(solution)/shard_map/ppermute | solution.py:117
  21.8 39.5 %collective-permute-start = (bf16[256,1792]{1,0:T(8,128)(2,1)}, bf16[256,1792]{1,0:T(8,128)(2,1)}, u32[]{:S(2)}, u32[]{:S(2)}) collective-permute-start(bf16[256,1792]{1,0:T(8,128)(2,1)} %get-tuple-element.79.refs_0_), channel_id=1, source_target_pairs={{0,4},{4,0},{8,12},{12,8},{16,20},{20,16},{24,28},{28,24},{1,5},{5... | collective-permute-start | bytes 2752520 | tf_op jit(solution)/shard_map/ppermute | solution.py:117
  79.8 19.9 %collective-permute-start.10 = (bf16[4,256,384]{2,1,0:T(8,128)(2,1)}, bf16[4,256,384]{2,1,0:T(8,128)(2,1)S(1)}, u32[]{:S(2)}, u32[]{:S(2)}) collective-permute-start(bf16[4,256,384]{2,1,0:T(8,128)(2,1)} %get-tuple-element.87), channel_id=1, source_target_pairs={{0,8},{4,12},{8,0},{12,4},{16,24},{20,28},{24,16},{28,20},{1,9},{5... | collective-permute-start | bytes 2359304 | tf_op jit(solution)/shard_map/ppermute | solution.py:117
  81.1 19.5 %collective-permute-start.11 = (bf16[4,256,384]{2,1,0:T(8,128)(2,1)}, bf16[4,256,384]{2,1,0:T(8,128)(2,1)S(1)}, u32[]{:S(2)}, u32[]{:S(2)}) collective-permute-start(bf16[4,256,384]{2,1,0:T(8,128)(2,1)} %get-tuple-element.89), channel_id=1, source_target_pairs={{0,16},{4,20},{8,24},{12,28},{16,0},{20,4},{24,8},{28,12},{1,17},{... | collective-permute-start | bytes 2359304 | tf_op jit(solution)/shard_map/ppermute | solution.py:117
  102.9 20.7 %collective-permute-start.12 = (bf16[2,256,384]{2,1,0:T(8,128)(2,1)S(1)}, bf16[2,256,384]{2,1,0:T(8,128)(2,1)S(1)}, u32[]{:S(2)}, u32[]{:S(2)}) collective-permute-start(bf16[2,256,384]{2,1,0:T(8,128)(2,1)S(1)} %get-tuple-element.91.refs_9_), channel_id=1, source_target_pairs={{0,16},{4,20},{8,24},{12,28},{16,0},{20,4},{24,8},{28,12},{1,17},{... | collective-permute-start | bytes 1179656 | tf_op jit(solution)/shard_map/ppermute | solution.py:117
  103.7 37.2 %collective-permute-start.18 = (bf16[4,256,384]{2,1,0:T(8,128)(2,1)}, bf16[4,256,384]{2,1,0:T(8,128)(2,1)}, u32[]{:S(2)}, u32[]{:S(2)}) collective-permute-start(bf16[4,256,384]{2,1,0:T(8,128)(2,1)} %get-tuple-element.97), channel_id=1, source_target_pairs={{0,8},{4,12},{8,0},{12,4},{16,24},{20,28},{24,16},{28,20},{1,9},{5... | collective-permute-start | bytes 2359304 | tf_op jit(solution)/shard_map/ppermute | solution.py:117
  105.2 35.7 %collective-permute-start.19 = (bf16[4,256,384]{2,1,0:T(8,128)(2,1)}, bf16[4,256,384]{2,1,0:T(8,128)(2,1)}, u32[]{:S(2)}, u32[]{:S(2)}) collective-permute-start(bf16[4,256,384]{2,1,0:T(8,128)(2,1)} %get-tuple-element.99), channel_id=1, source_target_pairs={{0,16},{4,20},{8,24},{12,28},{16,0},{20,4},{24,8},{28,12},{1,17},{... | collective-permute-start | bytes 2359304 | tf_op jit(solution)/shard_map/ppermute | solution.py:117
  105.7 27.1 %collective-permute-start.13 = (bf16[2,256,384]{2,1,0:T(8,128)(2,1)}, bf16[2,256,384]{2,1,0:T(8,128)(2,1)S(1)}, u32[]{:S(2)}, u32[]{:S(2)}) collective-permute-start(bf16[2,256,384]{2,1,0:T(8,128)(2,1)} %get-tuple-element.92), channel_id=1, source_target_pairs={{0,8},{4,12},{8,0},{12,4},{16,24},{20,28},{24,16},{28,20},{1,9},{5... | collective-permute-start | bytes 1179656 | tf_op jit(solution)/shard_map/ppermute | solution.py:117
  122.8 43.7 %collective-permute-start.26 = (bf16[4,256,384]{2,1,0:T(8,128)(2,1)}, bf16[4,256,384]{2,1,0:T(8,128)(2,1)S(1)}, u32[]{:S(2)}, u32[]{:S(2)}) collective-permute-start(bf16[4,256,384]{2,1,0:T(8,128)(2,1)} %get-tuple-element.105), channel_id=1, source_target_pairs={{0,8},{4,12},{8,0},{12,4},{16,24},{20,28},{24,16},{28,20},{1,9},{5... | collective-permute-start | bytes 2359304 | tf_op jit(solution)/shard_map/ppermute | solution.py:117
  123.6 42.8 %collective-permute-start.27 = (bf16[4,256,384]{2,1,0:T(8,128)(2,1)}, bf16[4,256,384]{2,1,0:T(8,128)(2,1)}, u32[]{:S(2)}, u32[]{:S(2)}) collective-permute-start(bf16[4,256,384]{2,1,0:T(8,128)(2,1)} %get-tuple-element.107), channel_id=1, source_target_pairs={{0,16},{4,20},{8,24},{12,28},{16,0},{20,4},{24,8},{28,12},{1,17},{... | collective-permute-start | bytes 2359304 | tf_op jit(solution)/shard_map/ppermute | solution.py:117
  144.2 18.3 %collective-permute-start.20 = (bf16[2,256,384]{2,1,0:T(8,128)(2,1)}, bf16[2,256,384]{2,1,0:T(8,128)(2,1)}, u32[]{:S(2)}, u32[]{:S(2)}) collective-permute-start(bf16[2,256,384]{2,1,0:T(8,128)(2,1)} %get-tuple-element.100), channel_id=1, source_target_pairs={{0,16},{4,20},{8,24},{12,28},{16,0},{20,4},{24,8},{28,12},{1,17},{... | collective-permute-start | bytes 1179656 | tf_op jit(solution)/shard_map/ppermute | solution.py:117
  166.3 25.1 %collective-permute-start.22 = (bf16[2,256,384]{2,1,0:T(8,128)(2,1)S(1)}, bf16[2,256,384]{2,1,0:T(8,128)(2,1)S(1)}, u32[]{:S(2)}, u32[]{:S(2)}) collective-permute-start(bf16[2,256,384]{2,1,0:T(8,128)(2,1)S(1)} %get-tuple-element.103), channel_id=1, source_target_pairs={{0,4},{4,0},{8,12},{12,8},{16,20},{20,16},{24,28},{28,24},{1,5},{5... | collective-permute-start | bytes 1179656 | tf_op jit(solution)/shard_map/ppermute | solution.py:117
  168.5 34.4 %collective-permute-start.28 = (bf16[2,256,384]{2,1,0:T(8,128)(2,1)}, bf16[2,256,384]{2,1,0:T(8,128)(2,1)S(1)}, u32[]{:S(2)}, u32[]{:S(2)}) collective-permute-start(bf16[2,256,384]{2,1,0:T(8,128)(2,1)} %get-tuple-element.108), channel_id=1, source_target_pairs={{0,16},{4,20},{8,24},{12,28},{16,0},{20,4},{24,8},{28,12},{1,17},{... | collective-permute-start | bytes 1179656 | tf_op jit(solution)/shard_map/ppermute | solution.py:117
  169.3 33.6 %collective-permute-start.29 = (bf16[2,256,384]{2,1,0:T(8,128)(2,1)}, bf16[2,256,384]{2,1,0:T(8,128)(2,1)S(1)}, u32[]{:S(2)}, u32[]{:S(2)}) collective-permute-start(bf16[2,256,384]{2,1,0:T(8,128)(2,1)} %get-tuple-element.109), channel_id=1, source_target_pairs={{0,8},{4,12},{8,0},{12,4},{16,24},{20,28},{24,16},{28,20},{1,9},{5... | collective-permute-start | bytes 1179656 | tf_op jit(solution)/shard_map/ppermute | solution.py:117
  170.8 20.6 %collective-permute-start.16 = (bf16[256,512]{1,0:T(8,128)(2,1)S(1)}, bf16[256,512]{1,0:T(8,128)(2,1)S(1)}, u32[]{:S(2)}, u32[]{:S(2)}) collective-permute-start(bf16[256,512]{1,0:T(8,128)(2,1)S(1)} %copy-done.21), channel_id=1, source_target_pairs={{0,16},{4,20},{8,24},{12,28},{16,0},{20,4},{24,8},{28,12},{1,17},{... | collective-permute-start | bytes 786440 | tf_op jit(solution)/shard_map/ppermute | solution.py:117
  171.3 20.1 %collective-permute-start.17 = (bf16[256,512]{1,0:T(8,128)(2,1)S(1)}, bf16[256,512]{1,0:T(8,128)(2,1)S(1)}, u32[]{:S(2)}, u32[]{:S(2)}) collective-permute-start(bf16[256,512]{1,0:T(8,128)(2,1)S(1)} %copy-done.21), channel_id=1, source_target_pairs={{0,24},{4,28},{8,16},{12,20},{16,8},{20,12},{24,0},{28,4},{1,25},{... | collective-permute-start | bytes 786440 | tf_op jit(solution)/shard_map/ppermute | solution.py:117
  257.0 21.3 %collective-permute-start.40 = (bf16[2,2,64,896]{3,2,1,0:T(8,128)(2,1)S(1)}, bf16[2,2,64,896]{3,2,1,0:T(8,128)(2,1)S(1)}, u32[]{:S(2)}, u32[]{:S(2)}) collective-permute-start(bf16[2,2,64,896]{3,2,1,0:T(8,128)(2,1)S(1)} %get-tuple-element.119.refs_0_), channel_id=1, source_target_pairs={{0,8},{4,12},{8,0},{12,4},{16,24},{20,28},{24,16},{28,20},{1,9},{5... | collective-permute-start | bytes 1376264 | tf_op jit(solution)/shard_map/ppermute | solution.py:117
  258.6 29.5 %collective-permute-start.42 = (bf16[2,2,64,896]{3,2,1,0:T(8,128)(2,1)S(1)}, bf16[2,2,64,896]{3,2,1,0:T(8,128)(2,1)S(1)}, u32[]{:S(2)}, u32[]{:S(2)}) collective-permute-start(bf16[2,2,64,896]{3,2,1,0:T(8,128)(2,1)S(1)} %get-tuple-element.120.refs_0_), channel_id=1, source_target_pairs={{0,8},{4,12},{8,0},{12,4},{16,24},{20,28},{24,16},{28,20},{1,9},{5... | collective-permute-start | bytes 1376264 | tf_op jit(solution)/shard_map/ppermute | solution.py:117
  270.2 26.9 %collective-permute-start.47 = (bf16[2,2,64,896]{3,2,1,0:T(8,128)(2,1)S(1)}, bf16[2,2,64,896]{3,2,1,0:T(8,128)(2,1)S(1)}, u32[]{:S(2)}, u32[]{:S(2)}) collective-permute-start(bf16[2,2,64,896]{3,2,1,0:T(8,128)(2,1)S(1)} %get-tuple-element.121.refs_0_), channel_id=1, source_target_pairs={{0,8},{4,12},{8,0},{12,4},{16,24},{20,28},{24,16},{28,20},{1,9},{5... | collective-permute-start | bytes 1376264 | tf_op jit(solution)/shard_map/ppermute | solution.py:117
  297.1 21.4 %collective-permute-start.49 = (bf16[2,2,64,896]{3,2,1,0:T(8,128)(2,1)S(1)}, bf16[2,2,64,896]{3,2,1,0:T(8,128)(2,1)S(1)}, u32[]{:S(2)}, u32[]{:S(2)}) collective-permute-start(bf16[2,2,64,896]{3,2,1,0:T(8,128)(2,1)S(1)} %get-tuple-element.137.refs_0_), channel_id=1, source_target_pairs={{0,1},{1,0},{2,3},{3,2},{4,5},{5,4},{6,7},{7,6},{8,9},{9,8},{10,11... | collective-permute-start | bytes 1376264 | tf_op jit(solution)/shard_map/ppermute | solution.py:117
  (94 other events, 1007.9 us)
where the time goes:
time: 348 us; the launch traced here: 344 us
  Pallas kernels  128 us (37%)
  waiting for transfers between devices  119 us (34%)
  starting transfers between devices  55.9 us (16%)
  local copies, waits for them, and re-layouts  33.9 us (10%)
  between operations  3.76 us (1%)
    ppermute x54, waiting for transfers between devices, swap(): return lax.ppermute(value, axis, [(i, i ^ mask) for i in range(size)])  119 us
    ppermute x54, starting transfers between devices, swap(): return lax.ppermute(value, axis, [(i, i ^ mask) for i in range(size)])  55.9 us
    pallas_call x3, Pallas kernels, project(): pl.pallas_call(functools.partial(project_kernel, blocks=blocks, group=gro...  42.8 us
    pallas_call x3, Pallas kernels, attend(): pl.pallas_call(functools.partial(attend_kernel, key_len=key_len, behind=l...  32.1 us
    unnamed x137, local copies, waits for them, and re-layouts  29.7 us
    pallas_call x1, Pallas kernels, weave(): pl.pallas_call(functools.partial(weave_kernel, cuts=cuts, behind=len(behi...  16.1 us
    pallas_call x1, Pallas kernels, output(): pl.pallas_call(functools.partial(output_kernel, pairs=pairs, groups=group...  8.81 us
    pallas_call x20, Pallas kernels, block_call(): pl.pallas_call(functools.partial(kernel, behind=len(behind)), out_shape=[...  7.95 us
  transfers between devices with their start and end apart: 54, of which 21 were waited for; matrix products, arithmetic and copies ran while one was open for 2% of the time, Pallas kernels for 30%

commit v1 on v0

--- a/solution.py
+++ b/solution.py
@@ -87,7 +87,7 @@
             in_specs=specs + [pl.BlockSpec(memory_space=pl.ANY)] * len(behind),
             out_specs=pl.BlockSpec((step, 3 * half), lambda side, i, meta: ((meta[0] ^ side) * steps + i, 0)),
         ),
-        compiler_params=pltpu.CompilerParams(vmem_limit_bytes=40 * MIB),
+        compiler_params=pltpu.CompilerParams(vmem_limit_bytes=60 * MIB),
         cost_estimate=SMALL,
     )(core.reshape(1).astype(jnp.int32), w_query, w_keyval, taken_query, taken_keyval, *behind)
 
@@ -109,6 +109,7 @@
         in_specs=[space] * (len(sources) + len(behind)),
         out_specs=[pl.BlockSpec(memory_space=pltpu.VMEM)] * len(sources),
         scratch_shapes=[pltpu.SemaphoreType.DMA((len(sources),))],
+        compiler_params=pltpu.CompilerParams(vmem_limit_bytes=60 * MIB),
         cost_estimate=SMALL,
     )(*sources, *behind)
 
@@ -204,7 +205,7 @@
         out_shape=[jax.ShapeDtypeStruct(shape, BF16) for shape in shapes],
         in_specs=specs + [pl.BlockSpec(memory_space=pl.ANY)] * len(behind),
         out_specs=[pl.BlockSpec(shape, lambda i: (0, 0, 0)) for shape in shapes],
-        compiler_params=pltpu.CompilerParams(vmem_limit_bytes=24 * MIB),
+        compiler_params=pltpu.CompilerParams(vmem_limit_bytes=60 * MIB),
         cost_estimate=SMALL,
     )(*[t for ts in terms for t in ts], *behind)
 
@@ -235,7 +236,7 @@
         + specs
         + [pl.BlockSpec(memory_space=pl.ANY)] * len(behind),
         out_specs=[whole, whole],
-        compiler_params=pltpu.CompilerParams(vmem_limit_bytes=24 * MIB),
+        compiler_params=pltpu.CompilerParams(vmem_limit_bytes=60 * MIB),
         cost_estimate=SMALL,
     )(bias, scale, *[t for ts in terms for t in ts], *behind)
 
@@ -357,7 +358,7 @@
         in_specs=[space] * (groups * pairs) + [vmem] * 2,
         out_specs=[vmem] * chunks,
         scratch_shapes=[pltpu.VMEM((pairs, rows, head_cols), BF16), pltpu.SemaphoreType.DMA((pairs,))],
-        compiler_params=pltpu.CompilerParams(vmem_limit_bytes=40 * MIB),
+        compiler_params=pltpu.CompilerParams(vmem_limit_bytes=60 * MIB),
         cost_estimate=SMALL,
     )(*[a for part in gathered for a in part], *w_pair)
 
@@ -375,7 +376,7 @@
                 pl.BlockSpec(shape, lambda i, meta, rank=len(shape): (0,) * rank) for shape in out_shapes
             ],
         ),
-        compiler_params=pltpu.CompilerParams(vmem_limit_bytes=16 * MIB),
+        compiler_params=pltpu.CompilerParams(vmem_limit_bytes=60 * MIB),
         cost_estimate=SMALL,
     )(scalars, *arrays, *behind)
 
@@ -501,8 +502,8 @@
     parts = [(g * per_group, (g + 1) * per_group) for g in range(groups)]
     taken = swap(w_query, "row", 1, rows_n), swap(w_keyval, "row", 1, rows_n)
     weights = weave(core, w_query, w_keyval, *taken, parts, [pieces[0]])
-    w_pair = w_out, swap(w_out, "row", 1, rows_n)
-    arrived = fetch(x_blocks[2::2], [weights, w_pair[1]])
+    w_pair = w_out, swap(fetch([w_out], [weights])[0], "row", 1, rows_n)
+    arrived = fetch(x_blocks[2::2], [weights])
     for offset in range(pairs):
         x_blocks[2 * offset + 1] = swap(arrived[offset - 1] if offset else x_blocks[0], "row", 1, rows_n)
 
@@ -532,7 +533,7 @@
         )
         came = swap(theirs, "row", 1, rows_n)
         attended, new_k, new_v = attend(
-            attend_meta, mine, came, cache_keys, cache_values, base, half, gathered[0][1:] if g == 1 else []
+            attend_meta, mine, came, cache_keys, cache_values, base, half, []
         )
         finished.append(attended)
         key_parts.append(new_k)
@@ -543,7 +544,7 @@
         terms = [[projected[g][2 * p]] for p in range(len(orders))]
         sends = [projected[g][2 * p + 1] for p in range(len(orders))]
         if g + 1 < groups:
-            projected.append(project_group(g + 1, [sent] if g else [projected[0][0]]))
+            projected.append(project_group(g + 1, [sent] if g else [projected[0][0], w_pair[1]]))
         for at in range(len(pair_bits)):
             for p, order in enumerate(orders):
                 terms[p].append(swap(sends[p], "row", 1 << order[at], rows_n))
@@ -572,7 +573,7 @@
     flips = [flip.reshape(1).astype(jnp.int32) for flip in flips]
     final_meta = jnp.stack([core, col]).astype(jnp.int32)
     late = [0, 0] + [at for bit in range(1, last) for at in (4.5 * bit + 1.5, 4.5 * bit + 4.5)]
-    late += [4.5 * last + 1.5, 4.5 * last + 4.6]
+    late += [4.5 * last + 1.5, 4.5 * last + 2.8]
     order = sorted((c * (2 if step > 1 else 0.5) + late[step], step, c) for c in range(chunks) for step in range(1, 2 * last + 2))
     products = output(gathered, w_pair, chunks)
     state = {c: (product, swap(product, "row", 1, rows_n)) for c, product in enumerate(products)}

time: 348 us -> 381 us (1.095)
  Pallas kernels: 128 us -> 182 us
  waiting for transfers between devices: 119 us -> 96.1 us
  local copies, waits for them, and re-layouts: 33.9 us -> 40 us
  starting transfers between devices: 55.9 us -> 49.9 us
    pallas_call x20, Pallas kernels: 7.95 us -> 47.5 us  [block_call(): pl.pallas_call(functools.partial(kernel, behind=len(behind)), out_shape=[...]
    ppermute x54, waiting for transfers between devices: 119 us -> 96.1 us  [swap(): return lax.ppermute(value, axis, [(i, i ^ mask) for i in range(size)])]
    ppermute x54, starting transfers between devices: 55.9 us -> 49.9 us  [swap(): return lax.ppermute(value, axis, [(i, i ^ mask) for i in range(size)])]
    pallas_call x3, Pallas kernels: 4.17 us -> 8.38 us  [settle(): pl.pallas_call(functools.partial(settle_kernel, parts=len(terms), terms=l...]
    pallas_call x1, Pallas kernels: 8.81 us -> 13 us  [output(): pl.pallas_call(functools.partial(output_kernel, pairs=pairs, groups=group...]
    unnamed x137 -> x143, local copies, waits for them, and re-layouts: 29.7 us -> 32.9 us
  transfers between devices with their start and end apart: 54 -> 54, of which waited for: 21 -> 20; matrix products, arithmetic and copies ran while one was open for 2% -> 5% of each run, Pallas kernels for 30% -> 37%
where the time goes in v1:
time: 381 us; the launch traced here: 377 us
  Pallas kernels  182 us (48%)
  waiting for transfers between devices  96.1 us (25%)
  starting transfers between devices  49.9 us (13%)
  local copies, waits for them, and re-layouts  40 us (10%)
  other arithmetic  5.66 us (1%)
    ppermute x54, waiting for transfers between devices, swap(): return lax.ppermute(value, axis, [(i, i ^ mask) for i in range(size)])  96.1 us
    ppermute x54, starting transfers between devices, swap(): return lax.ppermute(value, axis, [(i, i ^ mask) for i in range(size)])  49.9 us
    pallas_call x20, Pallas kernels, block_call(): pl.pallas_call(functools.partial(kernel, behind=len(behind)), out_shape=[...  47.5 us
    pallas_call x3, Pallas kernels, project(): pl.pallas_call(functools.partial(project_kernel, blocks=blocks, group=gro...  42.5 us
    unnamed x143, local copies, waits for them, and re-layouts  32.9 us
    pallas_call x3, Pallas kernels, attend(): pl.pallas_call(functools.partial(attend_kernel, key_len=key_len, behind=l...  31.9 us
    pallas_call x1, Pallas kernels, weave(): pl.pallas_call(functools.partial(weave_kernel, cuts=cuts, behind=len(behi...  16.8 us
    pallas_call x1, Pallas kernels, output(): pl.pallas_call(functools.partial(output_kernel, pairs=pairs, groups=group...  13 us
  transfers between devices with their start and end apart: 54, of which 20 were waited for; matrix products, arithmetic and copies ran while one was open for 5% of the time, Pallas kernels for 37%

profile of v1, /device:TPU:0, one launch (start us, length us, event | category | flops | bytes accessed | tf_op | source)
XLA Modules:
  0.0 376.8 jit_solution(5689608961446833102)
XLA Ops:
  1.2 7.8 %shard_map.148 = (bf16[256,1792]{1,0:T(8,128)(2,1)}, bf16[256,1792]{1,0:T(8,128)(2,1)}, bf16[256,1792]{1,0:T(8,128)(2,1)}, bf16[256,1792]{1,0:T(8,128)(2,1)}) custom-call(s32[1]{0:T(128)} %bitcast.8.meta_ref, bf16[256,7168]{1,0:T(8,128)(2,1)} %hidden_ref.9, f32[1,7168]{1,0:T(1,128)} %bitcast.20, f32[1,7168]{1,0:T(1,128)} %bitcast.21), custom_call_target="tpu_custom_call" | custom-call | flops 1 | bytes 1 | tf_op jit(solution)/shard_map/pallas_call | solution.py:35
  9.1 4.8 %collective-permute-done.4.taken_q_ref = bf16[896,1536]{1,0:T(8,128)(2,1)S(1)} collective-permute-done((bf16[896,1536]{1,0:T(8,128)(2,1)}, bf16[896,1536]{1,0:T(8,128)(2,1)S(1)}, u32[]{:S(2)}, u32[]{:S(2)}) %collective-permute-start.4) | collective-permute-done | bytes 2752544 | tf_op jit(solution)/shard_map/ppermute | solution.py:118
  15.4 16.8 %shard_map.149.refs_3_.refs_8_.refs_1_ = bf16[1792,2304]{1,0:T(8,128)(2,1)} custom-call(s32[1]{0:T(128)} %bitcast.meta_ref, bf16[896,1536]{1,0:T(8,128)(2,1)} %q_ref.1, bf16[896,2,1536]{2,1,0:T(2,128)(2,1)} %kv_ref.1, bf16[896,1536]{1,0:T(8,128)(2,1)} %copy-done.12, bf16[896,2,1536]{2,1,0:T(2,128)(2,1)} %collective-permute-done.5.taken_kv_ref, ...), custom_call_target="tpu_custom_call" | custom-call | flops 1 | bytes 1 | tf_op jit(solution)/shard_map/pallas_call | solution.py:81
  32.3 3.4 shard_map.152
  40.3 19.7 %collective-permute-done.1.refs_0_.refs_2_ = bf16[256,1792]{1,0:T(8,128)(2,1)S(1)} collective-permute-done((bf16[256,1792]{1,0:T(8,128)(2,1)}, bf16[256,1792]{1,0:T(8,128)(2,1)S(1)}, u32[]{:S(2)}, u32[]{:S(2)}) %collective-permute-start.1) | collective-permute-done | bytes 917536 | tf_op jit(solution)/shard_map/ppermute | solution.py:118
  60.0 20.6 %collective-permute-done.2.refs_1_.refs_4_ = bf16[256,1792]{1,0:T(8,128)(2,1)S(1)} collective-permute-done((bf16[256,1792]{1,0:T(8,128)(2,1)}, bf16[256,1792]{1,0:T(8,128)(2,1)S(1)}, u32[]{:S(2)}, u32[]{:S(2)}) %collective-permute-start.2) | collective-permute-done | bytes 917536 | tf_op jit(solution)/shard_map/ppermute | solution.py:118
  81.6 3.3 shard_map.150
  91.2 14.1 %shard_map.151 = (bf16[4,256,384]{2,1,0:T(8,128)(2,1)}, bf16[4,256,384]{2,1,0:T(8,128)(2,1)}, bf16[4,256,384]{2,1,0:T(8,128)(2,1)}, bf16[4,256,384]{2,1,0:T(8,128)(2,1)}) custom-call(s32[8]{0:T(128)} %broadcast_xor_fusion.meta_ref, bf16[256,1792]{1,0:T(8,128)(2,1)} %get-tuple-element.79.refs_0_, bf16[256,1792]{1,0:T(8,128)(2,1)} %collective-permute-done.refs_1_, ...), custom_call_target="tpu_custom_call" | custom-call | flops 1 | bytes 1 | tf_op jit(solution)/shard_map/pallas_call | solution.py:175
  107.4 14.1 %shard_map.153 = (bf16[4,256,384]{2,1,0:T(8,128)(2,1)}, bf16[4,256,384]{2,1,0:T(8,128)(2,1)}, bf16[4,256,384]{2,1,0:T(8,128)(2,1)}, bf16[4,256,384]{2,1,0:T(8,128)(2,1)}) custom-call(s32[8]{0:T(128)} %broadcast_xor_fusion.meta_ref, bf16[256,1792]{1,0:T(8,128)(2,1)} %get-tuple-element.79.refs_0_, bf16[256,1792]{1,0:T(8,128)(2,1)} %collective-permute-done.refs_1_, ...), custom_call_target="tpu_custom_call" | custom-call | flops 1 | bytes 1 | tf_op jit(solution)/shard_map/pallas_call | solution.py:175
  133.3 14.3 %shard_map.155 = (bf16[4,256,384]{2,1,0:T(8,128)(2,1)}, bf16[4,256,384]{2,1,0:T(8,128)(2,1)}, bf16[4,256,384]{2,1,0:T(8,128)(2,1)}, bf16[4,256,384]{2,1,0:T(8,128)(2,1)}) custom-call(s32[8]{0:T(128)} %broadcast_xor_fusion.meta_ref, bf16[256,1792]{1,0:T(8,128)(2,1)} %get-tuple-element.79.refs_0_, bf16[256,1792]{1,0:T(8,128)(2,1)} %collective-permute-done.refs_1_, ...), custom_call_target="tpu_custom_call" | custom-call | flops 1 | bytes 1 | tf_op jit(solution)/shard_map/pallas_call | solution.py:175
  155.8 4.0 %collective-permute-done.19.refs_3_.refs_4_ = bf16[4,256,384]{2,1,0:T(8,128)(2,1)S(1)} collective-permute-done((bf16[4,256,384]{2,1,0:T(8,128)(2,1)}, bf16[4,256,384]{2,1,0:T(8,128)(2,1)S(1)}, u32[]{:S(2)}, u32[]{:S(2)}) %collective-permute-start.19) | collective-permute-done | bytes 786464 | tf_op jit(solution)/shard_map/ppermute | solution.py:118
  169.1 10.6 %shard_map.157 = (bf16[256,512]{1,0:T(8,128)(2,1)}, bf16[256,512]{1,0:T(8,128)(2,1)}, bf16[256,512]{1,0:T(8,128)(2,1)}) custom-call(s32[2]{0:T(128)} %pad_add_fusion.1.meta_ref, bf16[2,256,384]{2,1,0:T(8,128)(2,1)} %get-tuple-element.94.own_ref, bf16[2,256,384]{2,1,0:T(8,128)(2,1)} %copy-done.35, bf16[1,4096,1536]{2,1,0:T(8,128)(2,1)} %k_ref.5, ...), custom_call_target="tpu_custom_call" | custom-call | flops 1 | bytes 1 | tf_op jit(solution)/shard_map/pallas_call | solution.py:301
  190.8 10.6 %shard_map.160 = (bf16[256,512]{1,0:T(8,128)(2,1)}, bf16[256,512]{1,0:T(8,128)(2,1)}, bf16[256,512]{1,0:T(8,128)(2,1)}) custom-call(s32[2]{0:T(128)} %pad_add_fusion.1.meta_ref, bf16[2,256,384]{2,1,0:T(8,128)(2,1)} %get-tuple-element.102.own_ref, bf16[2,256,384]{2,1,0:T(8,128)(2,1)} %copy-done.37, bf16[1,4096,1536]{2,1,0:T(8,128)(2,1)} %k_ref.5, ...), custom_call_target="tpu_custom_call" | custom-call | flops 1 | bytes 1 | tf_op jit(solution)/shard_map/pallas_call | solution.py:301
  210.6 10.8 %shard_map.163 = (bf16[256,512]{1,0:T(8,128)(2,1)}, bf16[256,512]{1,0:T(8,128)(2,1)}, bf16[256,512]{1,0:T(8,128)(2,1)}) custom-call(s32[2]{0:T(128)} %pad_add_fusion.1.meta_ref, bf16[2,256,384]{2,1,0:T(8,128)(2,1)} %get-tuple-element.110.own_ref, bf16[2,256,384]{2,1,0:T(8,128)(2,1)} %copy-done.36, bf16[1,4096,1536]{2,1,0:T(8,128)(2,1)} %k_ref.5, ...), custom_call_target="tpu_custom_call" | custom-call | flops 1 | bytes 1 | tf_op jit(solution)/shard_map/pallas_call | solution.py:301
  227.0 3.9 %collective-permute-done.24.refs_6_ = bf16[256,512]{1,0:T(8,128)(2,1)S(1)} collective-permute-done((bf16[256,512]{1,0:T(8,128)(2,1)S(1)}, bf16[256,512]{1,0:T(8,128)(2,1)S(1)}, u32[]{:S(2)}, u32[]{:S(2)}) %collective-permute-start.24) | collective-permute-done | bytes 262176 | tf_op jit(solution)/shard_map/ppermute | solution.py:118
  231.7 5.2 %collective-permute-done.31.refs_9_ = bf16[256,512]{1,0:T(8,128)(2,1)S(1)} collective-permute-done((bf16[256,512]{1,0:T(8,128)(2,1)}, bf16[256,512]{1,0:T(8,128)(2,1)S(1)}, u32[]{:S(2)}, u32[]{:S(2)}) %collective-permute-start.31) | collective-permute-done | bytes 262176 | tf_op jit(solution)/shard_map/ppermute | solution.py:118
  236.9 5.3 %collective-permute-done.32.refs_10_ = bf16[256,512]{1,0:T(8,128)(2,1)S(1)} collective-permute-done((bf16[256,512]{1,0:T(8,128)(2,1)}, bf16[256,512]{1,0:T(8,128)(2,1)S(1)}, u32[]{:S(2)}, u32[]{:S(2)}) %collective-permute-start.32) | collective-permute-done | bytes 262176 | tf_op jit(solution)/shard_map/ppermute | solution.py:118
  243.6 13.0 %shard_map.164 = (bf16[2,4,64,896]{3,2,1,0:T(8,128)(2,1)}, bf16[2,4,64,896]{3,2,1,0:T(8,128)(2,1)}, bf16[2,4,64,896]{3,2,1,0:T(8,128)(2,1)}, bf16[2,4,64,896]{3,2,1,0:T(8,128)(2,1)}) custom-call(bf16[256,512]{1,0:T(8,128)(2,1)} %get-tuple-element.96.refs_6_.refs_4_.refs_0_, bf16[256,512]{1,0:T(8,128)(2,1)} %copy-done.38, bf16[256,512]{1,0:T(8,128)(2,1)} %copy-done.39, ...), custom_call_target="tpu_custom_call" | custom-call | flops 1 | bytes 1 | tf_op jit(solution)/shard_map/pallas_call | solution.py:355
  291.8 5.3 %collective-permute-done.39.came_ref = bf16[2,2,64,896]{3,2,1,0:T(8,128)(2,1)S(1)} collective-permute-done((bf16[2,2,64,896]{3,2,1,0:T(8,128)(2,1)}, bf16[2,2,64,896]{3,2,1,0:T(8,128)(2,1)S(1)}, u32[]{:S(2)}, u32[]{:S(2)}) %collective-permute-start.39) | collective-permute-done | bytes 458784 | tf_op jit(solution)/shard_map/ppermute | solution.py:118
  325.7 3.4 collective-permute-start.51
  336.5 4.2 %collective-permute-done.47.came_ref = bf16[2,1,64,896]{3,2,1,0:T(8,128)(2,1)S(1)} collective-permute-done((bf16[2,1,64,896]{3,2,1,0:T(8,128)(2,1)}, bf16[2,1,64,896]{3,2,1,0:T(8,128)(2,1)S(1)}, u32[]{:S(2)}, u32[]{:S(2)}) %collective-permute-start.47) | collective-permute-done | bytes 229408 | tf_op jit(solution)/shard_map/ppermute | solution.py:118
  346.5 3.3 collective-permute-start.50
  353.3 3.2 collective-permute-done.50.came_ref
  363.6 7.5 %collective-permute-done.53.came_ref = bf16[2,1,64,896]{3,2,1,0:T(8,128)(2,1)S(1)} collective-permute-done((bf16[2,1,64,896]{3,2,1,0:T(8,128)(2,1)}, bf16[2,1,64,896]{3,2,1,0:T(8,128)(2,1)S(1)}, u32[]{:S(2)}, u32[]{:S(2)}) %collective-permute-start.53) | collective-permute-done | bytes 229408 | tf_op jit(solution)/shard_map/ppermute | solution.py:118
  (283 shorter events, 164.2 us)
Async XLA Ops:
  35.7 71.8 %collective-permute-start.11 = (bf16[1536,896]{1,0:T(8,128)(2,1)}, bf16[1536,896]{1,0:T(8,128)(2,1)}, u32[]{:S(2)}, u32[]{:S(2)}) collective-permute-start(bf16[1536,896]{1,0:T(8,128)(2,1)} %shard_map.152), channel_id=1, source_target_pairs={{0,4},{4,0},{8,12},{12,8},{16,20},{20,16},{24,28},{28,24},{1,5},{5... | collective-permute-start | bytes 8257544 | tf_op jit(solution)/shard_map/ppermute | solution.py:118
  35.9 24.2 %collective-permute-start.1 = (bf16[256,1792]{1,0:T(8,128)(2,1)}, bf16[256,1792]{1,0:T(8,128)(2,1)S(1)}, u32[]{:S(2)}, u32[]{:S(2)}) collective-permute-start(bf16[256,1792]{1,0:T(8,128)(2,1)} %get-tuple-element.80), channel_id=1, source_target_pairs={{0,8},{4,12},{8,0},{12,4},{16,24},{20,28},{24,16},{28,20},{1,9},{5... | collective-permute-start | bytes 2752520 | tf_op jit(solution)/shard_map/ppermute | solution.py:118
  38.7 42.0 %collective-permute-start.2 = (bf16[256,1792]{1,0:T(8,128)(2,1)}, bf16[256,1792]{1,0:T(8,128)(2,1)S(1)}, u32[]{:S(2)}, u32[]{:S(2)}) collective-permute-start(bf16[256,1792]{1,0:T(8,128)(2,1)} %get-tuple-element.81), channel_id=1, source_target_pairs={{0,16},{4,20},{8,24},{12,28},{16,0},{20,4},{24,8},{28,12},{1,17},{... | collective-permute-start | bytes 2752520 | tf_op jit(solution)/shard_map/ppermute | solution.py:118
  40.2 40.5 %collective-permute-start.3 = (bf16[256,1792]{1,0:T(8,128)(2,1)}, bf16[256,1792]{1,0:T(8,128)(2,1)}, u32[]{:S(2)}, u32[]{:S(2)}) collective-permute-start(bf16[256,1792]{1,0:T(8,128)(2,1)} %get-tuple-element.82), channel_id=1, source_target_pairs={{0,24},{4,28},{8,16},{12,20},{16,8},{20,12},{24,0},{28,4},{1,25},{... | collective-permute-start | bytes 2752520 | tf_op jit(solution)/shard_map/ppermute | solution.py:118
  40.2 46.7 %collective-permute-start = (bf16[256,1792]{1,0:T(8,128)(2,1)S(1)}, bf16[256,1792]{1,0:T(8,128)(2,1)}, u32[]{:S(2)}, u32[]{:S(2)}) collective-permute-start(bf16[256,1792]{1,0:T(8,128)(2,1)S(1)} %copy-done.1), channel_id=1, source_target_pairs={{0,4},{4,0},{8,12},{12,8},{16,20},{20,16},{24,28},{28,24},{1,5},{5... | collective-permute-start | bytes 2752520 | tf_op jit(solution)/shard_map/ppermute | solution.py:118
  105.3 19.9 %collective-permute-start.10 = (bf16[4,256,384]{2,1,0:T(8,128)(2,1)}, bf16[4,256,384]{2,1,0:T(8,128)(2,1)S(1)}, u32[]{:S(2)}, u32[]{:S(2)}) collective-permute-start(bf16[4,256,384]{2,1,0:T(8,128)(2,1)} %get-tuple-element.89), channel_id=1, source_target_pairs={{0,16},{4,20},{8,24},{12,28},{16,0},{20,4},{24,8},{28,12},{1,17},{... | collective-permute-start | bytes 2359304 | tf_op jit(solution)/shard_map/ppermute | solution.py:118
  106.9 20.6 %collective-permute-start.9 = (bf16[4,256,384]{2,1,0:T(8,128)(2,1)}, bf16[4,256,384]{2,1,0:T(8,128)(2,1)S(1)}, u32[]{:S(2)}, u32[]{:S(2)}) collective-permute-start(bf16[4,256,384]{2,1,0:T(8,128)(2,1)} %get-tuple-element.87), channel_id=1, source_target_pairs={{0,8},{4,12},{8,0},{12,4},{16,24},{20,28},{24,16},{28,20},{1,9},{5... | collective-permute-start | bytes 2359304 | tf_op jit(solution)/shard_map/ppermute | solution.py:118
  121.6 34.3 %collective-permute-start.18 = (bf16[4,256,384]{2,1,0:T(8,128)(2,1)}, bf16[4,256,384]{2,1,0:T(8,128)(2,1)S(1)}, u32[]{:S(2)}, u32[]{:S(2)}) collective-permute-start(bf16[4,256,384]{2,1,0:T(8,128)(2,1)} %get-tuple-element.97), channel_id=1, source_target_pairs={{0,8},{4,12},{8,0},{12,4},{16,24},{20,28},{24,16},{28,20},{1,9},{5... | collective-permute-start | bytes 2359304 | tf_op jit(solution)/shard_map/ppermute | solution.py:118
  130.7 18.4 %collective-permute-start.12 = (bf16[2,256,384]{2,1,0:T(8,128)(2,1)}, bf16[2,256,384]{2,1,0:T(8,128)(2,1)S(1)}, u32[]{:S(2)}, u32[]{:S(2)}) collective-permute-start(bf16[2,256,384]{2,1,0:T(8,128)(2,1)} %get-tuple-element.91.refs_9_), channel_id=1, source_target_pairs={{0,16},{4,20},{8,24},{12,28},{16,0},{20,4},{24,8},{28,12},{1,17},{... | collective-permute-start | bytes 1179656 | tf_op jit(solution)/shard_map/ppermute | solution.py:118
  131.2 28.6 %collective-permute-start.19 = (bf16[4,256,384]{2,1,0:T(8,128)(2,1)}, bf16[4,256,384]{2,1,0:T(8,128)(2,1)S(1)}, u32[]{:S(2)}, u32[]{:S(2)}) collective-permute-start(bf16[4,256,384]{2,1,0:T(8,128)(2,1)} %get-tuple-element.99), channel_id=1, source_target_pairs={{0,16},{4,20},{8,24},{12,28},{16,0},{20,4},{24,8},{28,12},{1,17},{... | collective-permute-start | bytes 2359304 | tf_op jit(solution)/shard_map/ppermute | solution.py:118
  132.8 20.2 %collective-permute-start.13 = (bf16[2,256,384]{2,1,0:T(8,128)(2,1)}, bf16[2,256,384]{2,1,0:T(8,128)(2,1)}, u32[]{:S(2)}, u32[]{:S(2)}) collective-permute-start(bf16[2,256,384]{2,1,0:T(8,128)(2,1)} %get-tuple-element.92), channel_id=1, source_target_pairs={{0,8},{4,12},{8,0},{12,4},{16,24},{20,28},{24,16},{28,20},{1,9},{5... | collective-permute-start | bytes 1179656 | tf_op jit(solution)/shard_map/ppermute | solution.py:118
  147.6 32.1 %collective-permute-start.26 = (bf16[4,256,384]{2,1,0:T(8,128)(2,1)}, bf16[4,256,384]{2,1,0:T(8,128)(2,1)S(1)}, u32[]{:S(2)}, u32[]{:S(2)}) collective-permute-start(bf16[4,256,384]{2,1,0:T(8,128)(2,1)} %get-tuple-element.105), channel_id=1, source_target_pairs={{0,8},{4,12},{8,0},{12,4},{16,24},{20,28},{24,16},{28,20},{1,9},{5... | collective-permute-start | bytes 2359304 | tf_op jit(solution)/shard_map/ppermute | solution.py:118
  149.2 30.5 %collective-permute-start.27 = (bf16[4,256,384]{2,1,0:T(8,128)(2,1)}, bf16[4,256,384]{2,1,0:T(8,128)(2,1)S(1)}, u32[]{:S(2)}, u32[]{:S(2)}) collective-permute-start(bf16[4,256,384]{2,1,0:T(8,128)(2,1)} %get-tuple-element.107), channel_id=1, source_target_pairs={{0,16},{4,20},{8,24},{12,28},{16,0},{20,4},{24,8},{28,12},{1,17},{... | collective-permute-start | bytes 2359304 | tf_op jit(solution)/shard_map/ppermute | solution.py:118
  163.1 20.1 %collective-permute-start.20 = (bf16[2,256,384]{2,1,0:T(8,128)(2,1)}, bf16[2,256,384]{2,1,0:T(8,128)(2,1)S(1)}, u32[]{:S(2)}, u32[]{:S(2)}) collective-permute-start(bf16[2,256,384]{2,1,0:T(8,128)(2,1)} %get-tuple-element.100), channel_id=1, source_target_pairs={{0,16},{4,20},{8,24},{12,28},{16,0},{20,4},{24,8},{28,12},{1,17},{... | collective-permute-start | bytes 1179656 | tf_op jit(solution)/shard_map/ppermute | solution.py:118
  163.6 19.6 %collective-permute-start.21 = (bf16[2,256,384]{2,1,0:T(8,128)(2,1)}, bf16[2,256,384]{2,1,0:T(8,128)(2,1)S(1)}, u32[]{:S(2)}, u32[]{:S(2)}) collective-permute-start(bf16[2,256,384]{2,1,0:T(8,128)(2,1)} %get-tuple-element.101), channel_id=1, source_target_pairs={{0,8},{4,12},{8,0},{12,4},{16,24},{20,28},{24,16},{28,20},{1,9},{5... | collective-permute-start | bytes 1179656 | tf_op jit(solution)/shard_map/ppermute | solution.py:118
  205.7 17.3 %collective-permute-start.16 = (bf16[256,512]{1,0:T(8,128)(2,1)S(1)}, bf16[256,512]{1,0:T(8,128)(2,1)S(1)}, u32[]{:S(2)}, u32[]{:S(2)}) collective-permute-start(bf16[256,512]{1,0:T(8,128)(2,1)S(1)} %copy-done.13), channel_id=1, source_target_pairs={{0,16},{4,20},{8,24},{12,28},{16,0},{20,4},{24,8},{28,12},{1,17},{... | collective-permute-start | bytes 786440 | tf_op jit(solution)/shard_map/ppermute | solution.py:118
  208.7 16.9 %collective-permute-start.23 = (bf16[256,512]{1,0:T(8,128)(2,1)S(1)}, bf16[256,512]{1,0:T(8,128)(2,1)S(1)}, u32[]{:S(2)}, u32[]{:S(2)}) collective-permute-start(bf16[256,512]{1,0:T(8,128)(2,1)S(1)} %copy-done.17), channel_id=1, source_target_pairs={{0,8},{4,12},{8,0},{12,4},{16,24},{20,28},{24,16},{28,20},{1,9},{5... | collective-permute-start | bytes 786440 | tf_op jit(solution)/shard_map/ppermute | solution.py:118
  209.2 21.6 %collective-permute-start.24 = (bf16[256,512]{1,0:T(8,128)(2,1)S(1)}, bf16[256,512]{1,0:T(8,128)(2,1)S(1)}, u32[]{:S(2)}, u32[]{:S(2)}) collective-permute-start(bf16[256,512]{1,0:T(8,128)(2,1)S(1)} %copy-done.17), channel_id=1, source_target_pairs={{0,16},{4,20},{8,24},{12,28},{16,0},{20,4},{24,8},{28,12},{1,17},{... | collective-permute-start | bytes 786440 | tf_op jit(solution)/shard_map/ppermute | solution.py:118
  223.8 18.4 %collective-permute-start.32 = (bf16[256,512]{1,0:T(8,128)(2,1)}, bf16[256,512]{1,0:T(8,128)(2,1)S(1)}, u32[]{:S(2)}, u32[]{:S(2)}) collective-permute-start(bf16[256,512]{1,0:T(8,128)(2,1)} %get-tuple-element.112.refs_8_), channel_id=1, source_target_pairs={{0,16},{4,20},{8,24},{12,28},{16,0},{20,4},{24,8},{28,12},{1,17},{... | collective-permute-start | bytes 786440 | tf_op jit(solution)/shard_map/ppermute | solution.py:118
  257.3 19.2 %collective-permute-start.36 = (bf16[2,4,64,896]{3,2,1,0:T(8,128)(2,1)}, bf16[2,4,64,896]{3,2,1,0:T(8,128)(2,1)S(1)}, u32[]{:S(2)}, u32[]{:S(2)}) collective-permute-start(bf16[2,4,64,896]{3,2,1,0:T(8,128)(2,1)} %get-tuple-element.116.own_ref), channel_id=1, source_target_pairs={{0,4},{4,0},{8,12},{12,8},{16,20},{20,16},{24,28},{28,24},{1,5},{5... | collective-permute-start | bytes 2752520 | tf_op jit(solution)/shard_map/ppermute | solution.py:118
  287.9 34.9 %collective-permute-start.46 = (bf16[2,2,64,896]{3,2,1,0:T(8,128)(2,1)}, bf16[2,2,64,896]{3,2,1,0:T(8,128)(2,1)S(1)}, u32[]{:S(2)}, u32[]{:S(2)}) collective-permute-start(bf16[2,2,64,896]{3,2,1,0:T(8,128)(2,1)} %get-tuple-element.121.refs_0_), channel_id=1, source_target_pairs={{0,8},{4,12},{8,0},{12,4},{16,24},{20,28},{24,16},{28,20},{1,9},{5... | collective-permute-start | bytes 1376264 | tf_op jit(solution)/shard_map/ppermute | solution.py:118
  291.4 21.1 %collective-permute-start.44 = (bf16[2,2,64,896]{3,2,1,0:T(8,128)(2,1)}, bf16[2,2,64,896]{3,2,1,0:T(8,128)(2,1)S(1)}, u32[]{:S(2)}, u32[]{:S(2)}) collective-permute-start(bf16[2,2,64,896]{3,2,1,0:T(8,128)(2,1)} %get-tuple-element.125.refs_0_), channel_id=1, source_target_pairs={{0,1},{1,0},{2,3},{3,2},{4,5},{5,4},{6,7},{7,6},{8,9},{9,8},{10,11... | collective-permute-start | bytes 1376264 | tf_op jit(solution)/shard_map/ppermute | solution.py:118
  305.1 27.3 %collective-permute-start.48 = (bf16[2,2,64,896]{3,2,1,0:T(8,128)(2,1)}, bf16[2,2,64,896]{3,2,1,0:T(8,128)(2,1)S(1)}, u32[]{:S(2)}, u32[]{:S(2)}) collective-permute-start(bf16[2,2,64,896]{3,2,1,0:T(8,128)(2,1)} %get-tuple-element.129.refs_0_), channel_id=1, source_target_pairs={{0,1},{1,0},{2,3},{3,2},{4,5},{5,4},{6,7},{7,6},{8,9},{9,8},{10,11... | collective-permute-start | bytes 1376264 | tf_op jit(solution)/shard_map/ppermute | solution.py:118
  325.7 24.1 %collective-permute-start.51 = (bf16[2,2,64,896]{3,2,1,0:T(8,128)(2,1)}, bf16[2,2,64,896]{3,2,1,0:T(8,128)(2,1)S(1)}, u32[]{:S(2)}, u32[]{:S(2)}) collective-permute-start(bf16[2,2,64,896]{3,2,1,0:T(8,128)(2,1)} %get-tuple-element.136.refs_0_), channel_id=1, source_target_pairs={{0,1},{1,0},{2,3},{3,2},{4,5},{5,4},{6,7},{7,6},{8,9},{9,8},{10,11... | collective-permute-start | bytes 1376264 | tf_op jit(solution)/shard_map/ppermute | solution.py:118
  (97 other events, 827.0 us)
